TPU v7x, 512 devices: a whole 4x4x16 slice. The times are simulated.
512 devices in a mesh: rows: 32 (over y, x, core), heads: 16 (over z).
Axes of the slice: x: 4, y: 4, z: 16, core: 2. Of those that a mesh axis runs over, the one named last changes fastest.
Arguments:
- pixels: float32 [8192, 768], P('rows'), may hold values from -6 to 6
- perturbation: float32 [8192, 768], P('rows'), may hold values from -0.6 to 0.6
- segment_ids: int32 [32, 256], P('rows'), may hold values from 0 to 3, never falling along the last dimension, each value on 1 to 128 neighbouring positions
- ball_radius: float32 [32, 4], P('rows'), may hold values from 0.05 to 0.4
- w_embed: bfloat16 [768, 1024], replicated, may hold values from -0.21875 to 0.21875
- gain_attn: float32 [1024], replicated, may hold values from 0.5 to 1.5
- w_qkv: bfloat16 [1024, 3, 1024], P('rows', None, 'heads'), may hold values from -0.1875 to 0.1875
- w_out: bfloat16 [1024, 1024], P('heads', 'rows'), may hold values from -0.1875 to 0.1875
- gain_mlp: float32 [1024], replicated, may hold values from 0.5 to 1.5
- w_up: bfloat16 [1024, 4096], P('rows', 'heads'), may hold values from -0.1875 to 0.1875
- w_down: bfloat16 [4096, 1024], P('heads', 'rows'), may hold values from -0.09375 to 0.09375
- out_grad: bfloat16 [8192, 1024], P('rows'), may hold values from -6 to 6
Outputs:
- block_out: bfloat16 [8192, 1024], P('rows')
- new_perturbation: float32 [8192, 768], P('rows')
Inputs may be any that keep to these rules, and one draw needn't show every extreme that they name: `segment_ids`: each pack numbers its images 0 to 3 in order along the pack; each image has 1 to 128 patches and some image of every pack has exactly 128.
All inputs are finite; a program needn't handle non-finite values.
Results may differ from a plain program's by a relative error of at most 0.019.
Values may be sent and summed in bfloat16 or wider, within the bound.
No kernel may reach another device: no remote copies, remote signals or barrier semaphores. Data moves between devices by JAX's collectives and lax.ppermute only.
A program may use at most 64 MiB of HBM per device.

v0:
```python
import math
import jax
import jax.numpy as jnp
from jax import lax
from jax.sharding import PartitionSpec as P

D = 1024
HEADS = 16
STEP_SIZE = 0.1


def layer_norm(values, gain):
    center = jnp.mean(values, -1, keepdims=True)
    shifted = values - center
    spread = jnp.mean(shifted * shifted, -1, keepdims=True)
    return shifted * lax.rsqrt(spread + 1e-05) * gain


def norm_back(values, gain, upstream):
    _, pull = jax.vjp(lambda t: layer_norm(t, gain), values)
    return pull(upstream)[0]


def gelu_back(values, upstream):
    _, pull = jax.vjp(jax.nn.gelu, values)
    return pull(upstream)[0]


def split_heads(projected):
    count, _, width = projected.shape
    size = D // HEADS
    parts = projected.reshape(count, 3, width // size, size)
    return (parts[:, 0], parts[:, 1], parts[:, 2])


def attend(projected, same):
    count, _, width = projected.shape
    query, keys, values = split_heads(projected)
    scale = 1.0 / math.sqrt(D // HEADS)
    scores = jnp.einsum("qhd,khd->hqk", query, keys, preferred_element_type=jnp.float32) * scale
    powers = jnp.where(same[None], jnp.exp(scores), 0.0)
    shares = powers / jnp.sum(powers, -1, keepdims=True)
    shares_low = shares.astype(jnp.bfloat16)
    mixed = jnp.einsum("hqk,khd->qhd", shares_low, values, preferred_element_type=jnp.float32)
    return (mixed.astype(jnp.bfloat16).reshape(count, width), shares, shares_low)


def attend_back(grad_heads, projected, shares, shares_low):
    count, _, width = projected.shape
    query, keys, values = split_heads(projected)
    size = D // HEADS
    scale = 1.0 / math.sqrt(size)
    upstream = grad_heads.reshape(count, width // size, size)
    grad_shares = jnp.einsum("qhd,khd->hqk", upstream, values, preferred_element_type=jnp.float32)
    grad_value = jnp.einsum(
        "hqk,qhd->khd", shares_low, upstream, preferred_element_type=jnp.float32
    ).astype(jnp.bfloat16)
    inner = jnp.sum(grad_shares * shares, -1, keepdims=True)
    grad_scores = (shares * (grad_shares - inner) * scale).astype(jnp.bfloat16)
    grad_query = jnp.einsum(
        "hqk,khd->qhd", grad_scores, keys, preferred_element_type=jnp.float32
    ).astype(jnp.bfloat16)
    grad_key = jnp.einsum(
        "hqk,qhd->khd", grad_scores, query, preferred_element_type=jnp.float32
    ).astype(jnp.bfloat16)
    return jnp.stack([grad_query, grad_key, grad_value], 1).reshape(count, 3, width)


def body(
    pixels,
    perturbation,
    segment_ids,
    ball_radius,
    w_embed,
    gain_attn,
    w_qkv,
    w_out,
    gain_mlp,
    w_up,
    w_down,
    out_grad,
):
    local_rows = pixels.shape[0]
    images = ball_radius.shape[1]
    patch_size = pixels.shape[1]
    w_qkv, w_out, w_up, w_down = (
        lax.all_gather(w_qkv, "rows", axis=0, tiled=True),
        lax.all_gather(w_out, "rows", axis=1, tiled=True),
        lax.all_gather(w_up, "rows", axis=0, tiled=True),
        lax.all_gather(w_down, "rows", axis=1, tiled=True),
    )
    model = w_qkv.shape[0]
    share = w_qkv.shape[2]
    labels = segment_ids[0]
    same = labels[:, None] == labels[None, :]
    inputs = (pixels + perturbation).astype(jnp.bfloat16)
    embedded = jnp.dot(inputs, w_embed, preferred_element_type=jnp.float32)
    normed_one = layer_norm(embedded, gain_attn).astype(jnp.bfloat16)
    projected = jnp.dot(
        normed_one, w_qkv.reshape(model, 3 * share), preferred_element_type=jnp.float32
    )
    projected = projected.reshape(local_rows, 3, share).astype(jnp.bfloat16)
    attended, shares, shares_low = attend(projected, same)
    attn_terms = jnp.dot(attended, w_out, preferred_element_type=jnp.float32)
    stream_mid = embedded + lax.psum(attn_terms.astype(jnp.bfloat16), "heads").astype(jnp.float32)
    normed_two = layer_norm(stream_mid, gain_mlp).astype(jnp.bfloat16)
    hidden_pre = jnp.dot(normed_two, w_up, preferred_element_type=jnp.float32)
    hidden_act = jax.nn.gelu(hidden_pre).astype(jnp.bfloat16)
    mlp_terms = jnp.dot(hidden_act, w_down, preferred_element_type=jnp.float32)
    stream_out = stream_mid + lax.psum(mlp_terms.astype(jnp.bfloat16), "heads").astype(jnp.float32)
    grad_hidden = jnp.dot(out_grad, w_down.T, preferred_element_type=jnp.float32)
    grad_pre = gelu_back(hidden_pre, grad_hidden).astype(jnp.bfloat16)
    up_terms = jnp.dot(grad_pre, w_up.T, preferred_element_type=jnp.float32)
    grad_norm_two = lax.psum(up_terms.astype(jnp.bfloat16), "heads").astype(jnp.float32)
    grad_mid = out_grad.astype(jnp.float32) + norm_back(stream_mid, gain_mlp, grad_norm_two)
    grad_mid_low = grad_mid.astype(jnp.bfloat16)
    grad_heads = jnp.dot(grad_mid_low, w_out.T, preferred_element_type=jnp.float32).astype(
        jnp.bfloat16
    )
    grad_proj = attend_back(grad_heads, projected, shares, shares_low)
    qkv_terms = jnp.einsum("tcf,dcf->td", grad_proj, w_qkv, preferred_element_type=jnp.float32)
    grad_norm_one = lax.psum(qkv_terms.astype(jnp.bfloat16), "heads").astype(jnp.float32)
    grad_embed = grad_mid + norm_back(embedded, gain_attn, grad_norm_one)
    grad_input = jnp.dot(
        grad_embed.astype(jnp.bfloat16), w_embed.T, preferred_element_type=jnp.float32
    )
    numbers = jnp.arange(images, dtype=jnp.int32)
    onehot = (labels[:, None] == numbers[None, :]).astype(jnp.float32)
    counts = jnp.sum(onehot, 0) * patch_size
    grad_sq = jnp.sum(onehot * jnp.sum(grad_input * grad_input, 1)[:, None], 0)
    scale = STEP_SIZE * lax.rsqrt(grad_sq / counts + 1e-06)
    candidate = perturbation + jnp.sum(onehot * scale[None, :], 1)[:, None] * grad_input
    cand_sq = jnp.sum(onehot * jnp.sum(candidate * candidate, 1)[:, None], 0)
    factor = jnp.minimum(1.0, ball_radius[0] * lax.rsqrt(cand_sq / counts + 1e-06))
    updated = candidate * jnp.sum(onehot * factor[None, :], 1)[:, None]
    return (stream_out.astype(jnp.bfloat16), updated)


def solution(mesh):
    in_specs = (
        P("rows", None),
        P("rows", None),
        P("rows", None),
        P("rows", None),
        P(),
        P(),
        P("rows", None, "heads"),
        P("heads", "rows"),
        P(),
        P("rows", "heads"),
        P("heads", "rows"),
        P("rows", None),
    )
    out_specs = (P("rows", None), P("rows", None))
    return jax.shard_map(body, mesh=mesh, in_specs=in_specs, out_specs=out_specs, check_vma=False)
```

profile of v0, /device:TPU:2, one launch (start us, length us, event | category | flops | bytes accessed | tf_op | source)
XLA Modules:
  0.0 501.0 jit_solution(2549400492572858672)
XLA Ops:
  7.2 0.0 copy-start
  7.2 0.0 copy-start.3
  7.2 0.0 all-reduce.5.cloned.1.call-start
  7.2 29.8 %all_gather.13 = bf16[64,1024]{0,1:T(8,128)(2,1)} all-gather(bf16[64,32]{0,1:T(8,128)(2,1)} %param.19), channel_id=1, replica_groups=mesh['rows'=32,'heads'=16] {'rows'}, dimensions={1}, use_global_device_ids=true | all-gather | bytes 135168 | tf_op jit(solution)/shard_map/all_gather | solution.py:88
  37.1 23.2 %all_gather.12 = bf16[1024,3,64]{2,0,1:T(8,128)(2,1)S(1)} all-gather(bf16[32,3,64]{2,0,1:T(8,128)(2,1)} %param.18), channel_id=1, replica_groups=mesh['rows'=32,'heads'=16] {'rows'}, dimensions={0}, use_global_device_ids=true | all-gather | bytes 405504 | tf_op jit(solution)/shard_map/all_gather | solution.py:87
  60.2 0.9 copy-done.4
  61.1 1.0 copy.15
  62.1 0.0 copy-done
  62.1 0.0 copy-done.3
  62.1 1.8 fusion.69
  64.0 0.0 copy-start.20
  64.0 0.2 multiply_reduce_fusion.3
  64.3 0.0 copy-start.24
  64.3 0.0 copy-done.11
  64.3 0.0 copy-done.17
  64.3 0.0 copy-start.22
  64.3 0.0 copy-start.18
  64.3 0.4 fusion.3
  64.7 0.0 copy-start.19
  64.7 1.6 fusion.70
  66.3 2.3 convolution_convert_fusion.2
  68.6 0.0 copy-done.22
  68.6 0.0 all-reduce.5.cloned.1.call-update
  68.6 0.0 all-reduce.7.cloned.1.call-start
  68.7 25.9 %all_gather.14 = bf16[1024,256]{1,0:T(8,128)(2,1)} all-gather(bf16[32,256]{1,0:T(8,128)(2,1)S(1)} %copy-done.18), channel_id=1, replica_groups=mesh['rows'=32,'heads'=16] {'rows'}, dimensions={0}, use_global_device_ids=true | all-gather | bytes 540672 | tf_op jit(solution)/shard_map/all_gather | solution.py:89
  94.6 0.0 copy-done.19
  94.6 25.3 %all_gather.15 = bf16[256,1024]{0,1:T(8,128)(2,1)} all-gather(bf16[256,32]{0,1:T(8,128)(2,1)S(1)} %copy-done.19), channel_id=1, replica_groups=mesh['rows'=32,'heads'=16] {'rows'}, dimensions={1}, use_global_device_ids=true | all-gather | bytes 540672 | tf_op jit(solution)/shard_map/all_gather | solution.py:90
  119.9 85.8 %all-reduce.5.cloned.1.call-done = bf16[256,1024]{1,0:T(8,128)(2,1)} async-done(((bf16[256,1024]{1,0:T(8,128)(2,1)}), bf16[256,1024]{1,0:T(8,128)(2,1)}) %all-reduce.5.cloned.1.call-update) | async-done | bytes 524304 | tf_op jit(solution)/shard_map/psum | solution.py:105
  205.6 1.3 fusion.68
  206.9 0.2 multiply_reduce_fusion.2
  207.2 0.7 copy-done.1
  207.9 1.1 fusion.12
  209.0 3.0 convolution_convert_fusion
  212.0 0.0 all-reduce.7.cloned.1.call-update
  212.0 0.2 all-reduce.9.cloned.1.call-start
  212.3 2.3 convolution_convert_fusion.1
  214.5 131.2 %all-reduce.7.cloned.1.call-done = bf16[256,1024]{1,0:T(8,128)(2,1)} async-done(((bf16[256,1024]{1,0:T(8,128)(2,1)}), bf16[256,1024]{1,0:T(8,128)(2,1)}) %all-reduce.7.cloned.1.call-update) | async-done | bytes 524304 | tf_op jit(solution)/shard_map/psum | solution.py:114
  345.7 1.8 multiply_reduce_fusion.1
  347.5 0.0 copy-start.13
  347.6 0.4 fusion.67
  348.0 0.5 copy-done.12
  348.5 0.2 copy-done.13
  348.6 0.4 convolution_convert_fusion.7
  349.0 0.1 copy-done.15
  349.2 0.2 fusion.7
  349.3 0.3 multiply_reduce_fusion.6
  349.6 0.0 copy-done.6
  349.7 0.2 fusion.6
  349.8 0.2 fusion.5
  350.0 0.3 copy-done.5
  350.3 1.3 fusion
  351.6 0.0 all-reduce.9.cloned.1.call-update
  351.6 135.9 %all-reduce.9.cloned.1.call-done = (bf16[256,1024]{1,0:T(8,128)(2,1)}, bf16[256,1024]{1,0:T(8,128)(2,1)}) async-done(((bf16[256,1024]{1,0:T(8,128)(2,1)}, bf16[256,1024]{1,0:T(8,128)(2,1)}), (bf16[256,1024]{1,0:T(8,128)(2,1)}, bf16[256,1024]{1,0:T(8,128)(2,1)})) %all-reduce.9.cloned.1.call-update) | async-done | bytes 1048592 | tf_op jit(solution)/shard_map/psum | solution.py:110
  487.4 2.7 multiply_reduce_fusion
  490.2 0.4 fusion.66
  490.6 0.7 copy-done.7
  491.4 0.1 copy-done.14
  491.5 1.0 multiply_reduce_fusion.5
  492.6 0.1 convert_reduce_fusion
  492.7 0.1 select_reduce_fusion.2
  492.8 0.3 multiply_reduce_fusion.4
  493.1 0.1 select_reduce_fusion.1
  493.2 0.1 select_reduce_fusion
  493.3 1.1 broadcast_multiply_fusion
  (44 shorter events, 0.2 us)
Async XLA Ops:
  7.2 55.0 %copy-start = (bf16[768,1024]{1,0:T(8,128)(2,1)S(1)}, bf16[768,1024]{1,0:T(8,128)(2,1)}, u32[]{:S(2)}) copy-start(bf16[768,1024]{1,0:T(8,128)(2,1)} %param.16) | copy-start | bytes 4718596
  7.2 55.0 %copy-start.3 = (f32[256,768]{1,0:T(8,128)S(1)}, f32[256,768]{1,0:T(8,128)}, u32[]{:S(2)}) copy-start(f32[256,768]{1,0:T(8,128)} %param.13) | copy-start | bytes 2359300
  7.2 198.4 %all-reduce.5.cloned.1.call-start = ((), (), s32[]{:S(2)}) async-start(), calls=%async_computation | async-start | bytes 1048576 | tf_op jit(solution)/shard_map/psum | solution.py:105
  60.2 0.9 copy-start.4
  62.1 2.1 copy-start.11
  62.1 2.2 copy-start.17
  64.0 0.7 copy-start.20
  64.3 2.0 copy-start.24
  64.3 4.3 copy-start.22
  64.3 4.4 copy-start.18
  64.7 29.9 %copy-start.19 = (bf16[256,32]{0,1:T(8,128)(2,1)S(1)}, bf16[256,32]{0,1:T(8,128)(2,1)}, u32[]{:S(2)}) copy-start(bf16[256,32]{0,1:T(8,128)(2,1)} %param.22) | copy-start | bytes 49156
  68.6 277.1 %all-reduce.7.cloned.1.call-start = ((), (), s32[]{:S(2)}) async-start(), calls=%async_computation.1 | async-start | bytes 1048576 | tf_op jit(solution)/shard_map/psum | solution.py:114
  119.8 88.1 %copy-start.16 = (f32[1024]{0:T(1024)S(1)}, f32[1024]{0:T(1024)}, u32[]{:S(2)}) copy-start(f32[1024]{0:T(1024)} %param.20) | copy-start | bytes 12292
  205.6 2.3 copy-start.10
  206.9 1.0 copy-start.1
  212.0 275.4 %all-reduce.9.cloned.1.call-start = ((), (), s32[]{:S(2)}) async-start(), calls=%async_computation.2 | async-start | bytes 2097152 | tf_op jit(solution)/shard_map/psum | solution.py:110
  345.7 1.8 copy-start.2
  345.7 1.8 copy-start.8
  347.5 1.0 copy-start.12
  347.5 1.1 copy-start.13
  348.0 1.6 copy-start.6
  348.0 1.2 copy-start.15
  348.0 1.2 copy-start.26
  349.1 1.1 copy-start.5
  487.4 2.7 copy-start.25
  487.4 2.7 copy-start.9
  487.4 2.8 copy-start.23
  490.2 1.2 copy-start.7
  490.2 1.4 copy-start.14
  491.5 1.0 copy-start.21
  492.5 0.7 copy-start.27
Sparse Core Ops, SparseCore 0:
  68.8 136.8 all-reduce.4
  212.2 133.5 all-reduce.6
  351.7 135.6 all-reduce.8
where the time goes:
time: 502 us; the launch traced here: 501 us
  waiting for transfers between devices  353 us (70%)
  blocking collectives  104 us (21%)
  matrix products  15.9 us (3%)
  between operations  14.1 us (3%)
  other arithmetic  9.03 us (2%)
    psum x1, waiting for transfers between devices, body(): lax.psum(mlp_terms.astype(jnp.bfloat16), 'heads').astype(jnp.float32)  136 us
    psum x1, waiting for transfers between devices, body(): lax.psum(up_terms.astype(jnp.bfloat16), 'heads').astype(jnp.float32)  131 us
    psum x1, waiting for transfers between devices, body(): lax.psum(attn_terms.astype(jnp.bfloat16), 'heads').astype(jnp.float32)  85.8 us
    all_gather x1, blocking collectives, body(): lax.all_gather(w_out, 'rows', axis=1, tiled=True)  29.8 us
    all_gather x1, blocking collectives, body(): lax.all_gather(w_up, 'rows', axis=0, tiled=True)  25.9 us
    all_gather x1, blocking collectives, body(): lax.all_gather(w_down, 'rows', axis=1, tiled=True)  25.3 us
    all_gather x1, blocking collectives, body(): lax.all_gather(w_qkv, 'rows', axis=0, tiled=True)  23.2 us
  transfers between devices with their start and end apart: 3, of which 3 were waited for; matrix products, arithmetic and copies ran while one was open for 0% of the time, Pallas kernels for 0%

commit v1 on v0

--- a/solution.py
+++ b/solution.py
@@ -107,7 +107,9 @@
     hidden_pre = jnp.dot(normed_two, w_up, preferred_element_type=jnp.float32)
     hidden_act = jax.nn.gelu(hidden_pre).astype(jnp.bfloat16)
     mlp_terms = jnp.dot(hidden_act, w_down, preferred_element_type=jnp.float32)
-    stream_out = stream_mid + lax.psum(mlp_terms.astype(jnp.bfloat16), "heads").astype(jnp.float32)
+    stream_out = stream_mid + jnp.sum(
+        lax.all_gather(mlp_terms.astype(jnp.bfloat16), "heads"), axis=0
+    ).astype(jnp.float32)
     grad_hidden = jnp.dot(out_grad, w_down.T, preferred_element_type=jnp.float32)
     grad_pre = gelu_back(hidden_pre, grad_hidden).astype(jnp.bfloat16)
     up_terms = jnp.dot(grad_pre, w_up.T, preferred_element_type=jnp.float32)

time: 502 us -> 611 us (1.22)
  waiting for transfers between devices: 353 us -> 455 us
  other arithmetic: 9.03 us -> 16.4 us
    all_gather x0 -> x1, waiting for transfers between devices: none -> 103 us  [body(): lax.all_gather(mlp_terms.astype(jnp.bfloat16), 'heads')]
    reduce_sum x0 -> x1, other arithmetic: none -> 6.34 us  [body(): jnp.sum(lax.all_gather(mlp_terms.astype(jnp.bfloat16), 'heads'), axis=0)]
  transfers between devices with their start and end apart: 3 -> 4, of which waited for: 3 -> 4; matrix products, arithmetic and copies ran while one was open for 0% -> 1% of each run, Pallas kernels for 0% -> 0%
where the time goes in v1:
time: 611 us; the launch traced here: 610 us
  waiting for transfers between devices  455 us (74%)
  blocking collectives  104 us (17%)
  other arithmetic  16.4 us (3%)
  matrix products  15.9 us (3%)
  between operations  14 us (2%)
    psum x1, waiting for transfers between devices, body(): lax.psum(qkv_terms.astype(jnp.bfloat16), 'heads').astype(jnp.float32)  135 us
    psum x1, waiting for transfers between devices, body(): lax.psum(up_terms.astype(jnp.bfloat16), 'heads').astype(jnp.float32)  131 us
    all_gather x1, waiting for transfers between devices, body(): lax.all_gather(mlp_terms.astype(jnp.bfloat16), 'heads')  103 us
    psum x1, waiting for transfers between devices, body(): lax.psum(attn_terms.astype(jnp.bfloat16), 'heads').astype(jnp.float32)  86.1 us
    all_gather x1, blocking collectives, body(): lax.all_gather(w_out, 'rows', axis=1, tiled=True)  30 us
    all_gather x1, blocking collectives, body(): lax.all_gather(w_up, 'rows', axis=0, tiled=True)  26.2 us
    all_gather x1, blocking collectives, body(): lax.all_gather(w_down, 'rows', axis=1, tiled=True)  24.9 us
    all_gather x1, blocking collectives, body(): lax.all_gather(w_qkv, 'rows', axis=0, tiled=True)  22.8 us
  transfers between devices with their start and end apart: 4, of which 4 were waited for; matrix products, arithmetic and copies ran while one was open for 1% of the time, Pallas kernels for 0%

profile of v1, /device:TPU:2, one launch (start us, length us, event | category | flops | bytes accessed | tf_op | source)
XLA Modules:
  0.0 610.1 jit_solution(10640472688989065488)
XLA Ops:
  7.2 0.0 copy-start
  7.2 0.0 copy-start.2
  7.2 0.0 all-reduce.4.cloned.1.call-start
  7.2 30.0 %all_gather.19 = bf16[64,1024]{0,1:T(8,128)(2,1)} all-gather(bf16[64,32]{0,1:T(8,128)(2,1)} %param.19), channel_id=1, replica_groups=mesh['rows'=32,'heads'=16] {'rows'}, dimensions={1}, use_global_device_ids=true | all-gather | bytes 135168 | tf_op jit(solution)/shard_map/all_gather | solution.py:88
  37.2 22.8 %all_gather.18 = bf16[1024,3,64]{2,0,1:T(8,128)(2,1)S(1)} all-gather(bf16[32,3,64]{2,0,1:T(8,128)(2,1)} %param.18), channel_id=1, replica_groups=mesh['rows'=32,'heads'=16] {'rows'}, dimensions={0}, use_global_device_ids=true | all-gather | bytes 405504 | tf_op jit(solution)/shard_map/all_gather | solution.py:87
  60.0 0.9 copy-done.3
  60.9 1.0 copy.15
  61.9 0.0 copy-done
  61.9 1.8 fusion.69
  63.8 0.0 copy-start.18
  63.8 0.2 multiply_reduce_fusion.3
  64.0 0.5 copy-done.21
  64.6 0.0 copy-done.9
  64.6 0.0 copy-start.16
  64.6 0.4 fusion.3
  65.0 0.0 copy-start.17
  65.0 1.5 fusion.70
  66.5 2.3 convolution_convert_fusion.2
  68.9 0.0 all-reduce.4.cloned.1.call-update
  68.9 0.0 all-reduce.6.cloned.1.call-start
  69.0 0.0 copy-done.16
  69.0 26.2 %all_gather.20 = bf16[1024,256]{1,0:T(8,128)(2,1)} all-gather(bf16[32,256]{1,0:T(8,128)(2,1)S(1)} %copy-done.16), channel_id=1, replica_groups=mesh['rows'=32,'heads'=16] {'rows'}, dimensions={0}, use_global_device_ids=true | all-gather | bytes 540672 | tf_op jit(solution)/shard_map/all_gather | solution.py:89
  95.2 24.9 %all_gather.21 = bf16[256,1024]{0,1:T(8,128)(2,1)} all-gather(bf16[256,32]{0,1:T(8,128)(2,1)S(1)} %copy-done.17), channel_id=1, replica_groups=mesh['rows'=32,'heads'=16] {'rows'}, dimensions={1}, use_global_device_ids=true | all-gather | bytes 540672 | tf_op jit(solution)/shard_map/all_gather | solution.py:90
  120.1 86.1 %all-reduce.4.cloned.1.call-done = bf16[256,1024]{1,0:T(8,128)(2,1)} async-done(((bf16[256,1024]{1,0:T(8,128)(2,1)}), bf16[256,1024]{1,0:T(8,128)(2,1)}) %all-reduce.4.cloned.1.call-update) | async-done | bytes 524304 | tf_op jit(solution)/shard_map/psum | solution.py:105
  206.2 1.3 fusion.68
  207.5 0.2 multiply_reduce_fusion.2
  207.8 0.8 copy-done.1
  208.5 0.0 copy-done.8
  208.6 1.1 fusion.12
  209.6 3.0 convolution_convert_fusion
  212.6 0.0 all-reduce.6.cloned.1.call-update
  212.7 0.0 all-gather.3.cloned.1.call-start
  212.7 2.3 convolution_convert_fusion.1
  215.0 0.0 all-gather.3.cloned.1.call-update
  215.0 0.2 all-reduce.8.cloned.1.call-start
  215.2 131.1 %all-reduce.6.cloned.1.call-done = bf16[256,1024]{1,0:T(8,128)(2,1)} async-done(((bf16[256,1024]{1,0:T(8,128)(2,1)}), bf16[256,1024]{1,0:T(8,128)(2,1)}) %all-reduce.6.cloned.1.call-update) | async-done | bytes 524304 | tf_op jit(solution)/shard_map/psum | solution.py:116
  346.3 1.7 multiply_reduce_fusion.1
  348.0 103.1 %all-gather.3.cloned.1.call-done = bf16[4096,1024]{1,0:T(8,128)(2,1)} async-done(((bf16[256,1024]{1,0:T(8,128)(2,1)}), bf16[4096,1024]{1,0:T(8,128)(2,1)}) %all-gather.3.cloned.1.call-update) | async-done | bytes 8388624 | tf_op jit(solution)/shard_map/all_gather | solution.py:111
  451.1 6.3 %reduce_sum.170 = bf16[256,1024]{1,0:T(8,128)(2,1)} reduce(bf16[16,256,1024]{2,1,0:T(8,128)(2,1)} %bitcast.88, bf16[]{:T(256)} %constant.36.clone.1), dimensions={0}, to_apply=%region_6.7 | reduce | flops 3932160 | bytes 8912898 | tf_op jit(solution)/shard_map/reduce_sum | solution.py:110
  457.5 2.8 fusion.67
  460.3 0.0 copy-done.10
  460.3 0.0 copy-done.11
  460.3 0.4 convolution_convert_fusion.7
  460.7 0.7 copy-done.13
  461.4 0.0 copy-done.23
  461.4 0.2 fusion.7
  461.5 0.3 multiply_reduce_fusion.6
  461.8 0.0 copy-done.5
  461.8 0.1 multiply_convert_fusion.3
  461.9 0.2 fusion.6
  462.1 0.2 fusion.5
  462.2 0.3 copy-done.4
  462.5 1.3 fusion
  463.8 0.0 all-reduce.8.cloned.1.call-update
  463.8 134.9 %all-reduce.8.cloned.1.call-done = bf16[256,1024]{1,0:T(8,128)(2,1)} async-done(((bf16[256,1024]{1,0:T(8,128)(2,1)}), bf16[256,1024]{1,0:T(8,128)(2,1)}) %all-reduce.8.cloned.1.call-update) | async-done | bytes 524304 | tf_op jit(solution)/shard_map/psum | solution.py:124
  598.7 1.5 multiply_reduce_fusion
  600.2 0.4 fusion.66
  600.6 1.0 multiply_reduce_fusion.5
  601.7 0.1 convert_reduce_fusion
  601.8 0.1 select_reduce_fusion.2
  601.9 0.3 multiply_reduce_fusion.4
  602.2 0.1 select_reduce_fusion.1
  602.4 0.1 select_reduce_fusion
  602.5 1.1 broadcast_multiply_fusion
  (42 shorter events, 0.1 us)
Async XLA Ops:
  7.2 54.7 %copy-start = (bf16[768,1024]{1,0:T(8,128)(2,1)S(1)}, bf16[768,1024]{1,0:T(8,128)(2,1)}, u32[]{:S(2)}) copy-start(bf16[768,1024]{1,0:T(8,128)(2,1)} %param.16) | copy-start | bytes 4718596
  7.2 54.7 %copy-start.2 = (f32[256,768]{1,0:T(8,128)S(1)}, f32[256,768]{1,0:T(8,128)}, u32[]{:S(2)}) copy-start(f32[256,768]{1,0:T(8,128)} %param.13) | copy-start | bytes 2359300
  7.2 199.0 %all-reduce.4.cloned.1.call-start = ((), (), s32[]{:S(2)}) async-start(), calls=%async_computation | async-start | bytes 1048576 | tf_op jit(solution)/shard_map/psum | solution.py:105
  60.0 0.9 copy-start.3
  61.9 2.7 copy-start.9
  61.9 2.7 copy-start.15
  63.8 1.3 copy-start.18
  64.0 0.5 copy-start.21
  64.6 4.3 copy-start.19
  64.6 4.4 copy-start.16
  65.0 30.2 %copy-start.17 = (bf16[256,32]{0,1:T(8,128)(2,1)S(1)}, bf16[256,32]{0,1:T(8,128)(2,1)}, u32[]{:S(2)}) copy-start(bf16[256,32]{0,1:T(8,128)(2,1)} %param.22) | copy-start | bytes 49156
  68.9 277.4 %all-reduce.6.cloned.1.call-start = ((), (), s32[]{:S(2)}) async-start(), calls=%async_computation.1 | async-start | bytes 1048576 | tf_op jit(solution)/shard_map/psum | solution.py:116
  120.1 88.4 %copy-start.14 = (f32[1024]{0:T(1024)S(1)}, f32[1024]{0:T(1024)}, u32[]{:S(2)}) copy-start(f32[1024]{0:T(1024)} %param.20) | copy-start | bytes 12292
  206.2 2.4 copy-start.8
  207.5 1.1 copy-start.1
  212.7 238.5 %all-gather.3.cloned.1.call-start = ((), (), s32[]{:S(2)}) async-start(), calls=%async_computation.3 | async-start | bytes 8912896 | tf_op jit(solution)/shard_map/all_gather | solution.py:111
  215.0 383.7 %all-reduce.8.cloned.1.call-start = ((), (), s32[]{:S(2)}) async-start(), calls=%async_computation.2 | async-start | bytes 1048576 | tf_op jit(solution)/shard_map/psum | solution.py:124
  457.5 2.8 copy-start.10
  457.5 2.8 copy-start.11
  460.3 1.6 copy-start.5
  460.3 1.1 copy-start.13
  460.3 1.1 copy-start.23
  461.4 1.1 copy-start.4
  462.5 137.6 %copy-start.22 = (f32[256]{0:T(256)S(1)}, f32[256]{0:T(256)}, u32[]{:S(2)}) copy-start(f32[256]{0:T(256)} %copy-done.21) | copy-start | bytes 3076
  462.5 137.7 %copy-start.20 = (f32[256]{0:T(256)S(1)}, f32[256]{0:T(256)}, u32[]{:S(2)}) copy-start(f32[256]{0:T(256)} %copy-done.19) | copy-start | bytes 3076
  598.7 1.5 copy-start.7
  598.7 2.0 copy-start.6
  598.7 2.0 copy-start.12
  601.7 0.7 copy-start.24
Sparse Core Ops, SparseCore 0:
  69.0 137.1 all-reduce.3
  212.8 133.5 all-reduce.5
  348.4 102.6 all-gather.2
  463.9 134.6 all-reduce.7
